TPU v7x, 32 devices: a whole 2x2x4 slice. The times are simulated.
32 devices in a mesh: wide: 32 (over z, y, x, core), narrow: 1.
Axes of the slice: x: 2, y: 2, z: 4, core: 2. Of those that a mesh axis runs over, the one named last changes fastest.
Arguments:
- integrals: bfloat16 [2048, 128, 128], P('narrow', 'wide'), may hold values from -6 to 6
- fitted: bfloat16 [2048, 128, 128], P('narrow', 'wide'), may hold values from -0.00390625 to 0.00390625
- occupied: bfloat16 [128, 1024], P('wide'), may hold values from -0.5 to 0.5
- pattern: int32 [8, 8], replicated, may hold values 0 or 1
Outputs:
- exchange_matrix: float32 [128, 128], P('wide')
All inputs are finite; a program needn't handle non-finite values.
Results may differ from a plain program's by a relative error of at most 0.0018.
Values may be sent and summed in bfloat16 or wider, within the bound.
No kernel may reach another device: no remote copies, remote signals or barrier semaphores. Data moves between devices by JAX's collectives and lax.ppermute only.
A program may use at most 64 MiB of HBM per device.

v0:
```python
import functools

import jax
import jax.numpy as jnp
import numpy as np
from jax import lax
from jax.experimental import pallas as pl
from jax.experimental.pallas import tpu as pltpu
from jax.sharding import PartitionSpec as P

NBLK = 8
FULL = NBLK // 2
DEPTH = 2048
VMEM = 62 * 2**20
SORT_VMEM = 24 * 2**20
NT = (((1,), (1,)), ((), ()))
PLANES = NBLK // 2
PLANS = ((4, 1), (5, 0), (4, 2), (5, 1), (6, 0), (5, 2), (8, 0))


def parts_of(cap, groups):
    parts = []
    for piece in (FULL, FULL, FULL // 2, FULL // 4):
        if cap >= piece and FULL // piece <= groups:
            parts.append(piece)
            cap -= piece
    return parts if cap == 0 else None


def with_extra(parts, extra):
    return list(parts) + [extra] * (extra > 0)


def lane_layout(parts, extra, basis):
    width = basis // NBLK
    lane = np.arange(basis)
    slot, base, offset = [], [], 0
    for piece in with_extra(parts, extra):
        inner = lane % (basis * piece // FULL)
        slot.append(offset + inner % (piece * width) // width)
        base.append(inner // (piece * width) * basis + inner % width)
        offset += piece
    slot = np.concatenate(slot)
    return np.stack([slot, np.concatenate(base), slot >= sum(parts)]).astype(np.int32)


def surplus(pattern_ref, block, direct):
    alive = jnp.int32(0)
    for other in range(NBLK):
        alive = alive + (pattern_ref[block, other] != 0).astype(jnp.int32)
    return jnp.maximum(alive - direct, 0)


def columns_of(pattern_ref, block, slot, base, width):
    columns = jnp.full(slot.shape, -1, jnp.int32)
    rank = jnp.int32(0)
    for other in range(NBLK):
        alive = pattern_ref[block, other] != 0
        columns = jnp.where(slot == jnp.where(alive, rank, -1), base + other * width, columns)
        rank = rank + alive.astype(jnp.int32)
    return columns


def halves(wide):
    high = wide.astype(jnp.bfloat16)
    return high, (wide - high.astype(jnp.float32)).astype(jnp.bfloat16)


def pack_kernel(parts, extra, groups, me_ref, pattern_ref, layout_ref, ints_hbm, fitted_hbm, *refs):
    out_hbm, over_hbm, (both, out, table, in_sems, out_sems) = refs[0], refs[1:-5], refs[-5:]
    count, rows, lanes = both.shape
    basis = lanes // 2
    chunks = count // PLANES
    step = rows // groups
    direct_rows = out_hbm.shape[1]
    extra_rows = out.shape[1] - direct_rows
    place = lax.rem(me_ref[0], chunks)

    def arrivals(turn):
        here = pl.ds(turn * chunks, chunks)
        return (
            pltpu.make_async_copy(ints_hbm.at[here], both.at[here, :, pl.ds(0, basis)], in_sems.at[turn, 0]),
            pltpu.make_async_copy(fitted_hbm.at[here], both.at[here, :, pl.ds(basis, basis)], in_sems.at[turn, 1]),
        )

    def departures(turn):
        here = pl.ds(turn * chunks, chunks)
        copies = [pltpu.make_async_copy(out.at[here, pl.ds(0, direct_rows)], out_hbm.at[here], out_sems.at[turn, 0])]
        for apart, ref in enumerate(over_hbm):
            source = out.at[turn * chunks + lax.bitwise_xor(place, apart), pl.ds(direct_rows, extra_rows)]
            copies.append(pltpu.make_async_copy(source, ref.at[turn], out_sems.at[turn, 1 + apart]))
        return copies

    for turn in range(PLANES):
        for copy in arrivals(turn):
            copy.start()

    layout = layout_ref[...]
    block = lax.div(me_ref[0] * NBLK, count)
    columns = columns_of(pattern_ref, block, layout[0:1], layout[1:2], basis // NBLK)
    height = lax.broadcasted_iota(jnp.int32, table.shape, 0)
    table[...] = jnp.where(height == columns, 1.0, 0.0).astype(jnp.bfloat16)

    lane = lax.broadcasted_iota(jnp.int32, (chunks * step, basis), 1)

    def work(turn, _):
        for copy in arrivals(turn):
            copy.wait()
        here = pl.ds(turn * chunks, chunks)
        packed = []
        for group in range(groups):
            mine = both[here, pl.ds(group * step, step), :].reshape(chunks * step, lanes)
            packed.append(jnp.dot(mine, table[...], preferred_element_type=jnp.float32))
        start = 0
        for index, piece in enumerate(with_extra(parts, extra)):
            shared = FULL // piece
            held = slice(index * basis, (index + 1) * basis)
            for inner in range(groups // shared):
                total = packed[inner][:, held]
                for other in range(1, shared):
                    theirs = packed[other * (groups // shared) + inner][:, held]
                    total = jnp.where(lane >= other * (basis // shared), theirs, total)
                out[here, pl.ds(start, step), :] = total.astype(jnp.bfloat16).reshape(chunks, step, basis)
                start += step
        for copy in departures(turn):
            copy.start()
        return 0

    lax.fori_loop(0, PLANES, work, 0)
    for turn in range(PLANES):
        for copy in departures(turn):
            copy.wait()


def pack(ints, fitted, me, pattern, parts, extra, groups):
    count, rows, basis = ints.shape
    direct_rows = sum(rows * piece // FULL for piece in parts)
    extra_rows = rows * extra // FULL
    plane = count // PLANES
    layout = lane_layout(parts, extra, basis)
    flops = 2 * count * rows * 2 * basis * layout.shape[1]
    moved = 2 * ints.nbytes + 2 * count * (direct_rows + extra_rows) * basis
    shapes = [jax.ShapeDtypeStruct((count, direct_rows, basis), jnp.bfloat16)]
    if extra:
        shapes += [jax.ShapeDtypeStruct((PLANES, extra_rows, basis), jnp.bfloat16)] * plane
    return pl.pallas_call(
        functools.partial(pack_kernel, parts, extra, groups),
        out_shape=shapes,
        in_specs=[
            pl.BlockSpec(memory_space=pltpu.SMEM),
            pl.BlockSpec(memory_space=pltpu.SMEM),
            pl.BlockSpec(memory_space=pltpu.VMEM),
            pl.BlockSpec(memory_space=pl.ANY),
            pl.BlockSpec(memory_space=pl.ANY),
        ],
        out_specs=[pl.BlockSpec(memory_space=pl.ANY)] * len(shapes),
        scratch_shapes=[
            pltpu.VMEM((count, rows, 2 * basis), jnp.bfloat16),
            pltpu.VMEM((count, direct_rows + extra_rows, basis), jnp.bfloat16),
            pltpu.VMEM((2 * basis, layout.shape[1]), jnp.bfloat16),
            pltpu.SemaphoreType.DMA((PLANES, 2)),
            pltpu.SemaphoreType.DMA((PLANES, len(shapes))),
        ],
        compiler_params=pltpu.CompilerParams(vmem_limit_bytes=VMEM),
        cost_estimate=pl.CostEstimate(flops=flops, bytes_accessed=moved, transcendentals=0),
        name="pack",
    )(me, pattern, jnp.asarray(layout), ints, fitted)


def sort_kernel(direct, me_ref, pattern_ref, slot_ref, over_ref, out_ref):
    planes, sources, _, basis = out_ref.shape
    plane = 2 * sources
    place, level = lax.rem(me_ref[0], plane), lax.div(me_ref[0], plane)
    first = surplus(pattern_ref, 2 * level, direct)
    row = lax.broadcasted_iota(jnp.int32, (basis, basis), 0)
    column = lax.broadcasted_iota(jnp.int32, (basis, basis), 1)
    slot = slot_ref[0:1]
    stay = jnp.where((row == column) & (slot < first), 1.0, 0.0)
    move = jnp.where((row == column - first * (basis // NBLK)) & (slot >= first), 1.0, 0.0)
    table = jnp.concatenate([stay, move], axis=0).astype(jnp.bfloat16)

    def work(away, _):
        there = lax.bitwise_xor(level, away)
        for source in range(sources):
            pair = [over_ref[lax.bitwise_xor(place, second * sources + source), there] for second in range(2)]
            sorted_rows = jnp.dot(jnp.concatenate(pair, axis=1), table, preferred_element_type=jnp.float32)
            out_ref[away, source] = sorted_rows.astype(jnp.bfloat16)
        return 0

    lax.fori_loop(0, planes, work, 0)


def sort(over, me, pattern, direct, extra):
    plane, _, rows, basis = over.shape
    slots = lane_layout((extra,), 0, basis)
    flops = 4 * PLANES * plane // 2 * rows * basis * basis
    return pl.pallas_call(
        functools.partial(sort_kernel, direct),
        out_shape=jax.ShapeDtypeStruct((PLANES, plane // 2, rows, basis), jnp.bfloat16),
        in_specs=[pl.BlockSpec(memory_space=pltpu.SMEM)] * 2 + [pl.BlockSpec(memory_space=pltpu.VMEM)] * 2,
        out_specs=pl.BlockSpec(memory_space=pltpu.VMEM),
        compiler_params=pltpu.CompilerParams(vmem_limit_bytes=SORT_VMEM),
        cost_estimate=pl.CostEstimate(flops=flops, bytes_accessed=2 * over.nbytes, transcendentals=0),
        name="sort",
    )(me, pattern, jnp.asarray(slots), over)


def weights_kernel(direct, pattern_ref, layout_ref, panel_ref, out_ref):
    basis = panel_ref.shape[0]
    lanes = layout_ref.shape[0]
    panel = panel_ref[...]
    gram = lax.dot_general(panel, panel, NT, preferred_element_type=jnp.float32)
    high, low = halves(gram)
    column = lax.broadcasted_iota(jnp.int32, (lanes, 2 * basis), 1)

    def fill(block, _):
        before = lax.rem(block, 2) * surplus(pattern_ref, block - lax.rem(block, 2), direct)
        slot = layout_ref[:, 0:1] - layout_ref[:, 2:3] * before
        slot = jnp.where((layout_ref[:, 2:3] == 0) | (slot >= direct), slot, -2)
        held = columns_of(pattern_ref, block, slot, layout_ref[:, 1:2], basis // NBLK)
        table = jnp.where(column == held, 1.0, 0.0).astype(jnp.bfloat16)
        ints = table[:, :basis]
        out_ref[block, :lanes, :basis] = jnp.dot(ints, high, preferred_element_type=jnp.float32).astype(jnp.bfloat16)
        out_ref[block, :lanes, basis:] = table[:, basis:]
        out_ref[block, lanes:, :basis] = jnp.dot(ints, low, preferred_element_type=jnp.float32).astype(jnp.bfloat16)
        out_ref[block, lanes:, basis:] = jnp.zeros((lanes, basis), jnp.bfloat16)
        return 0

    lax.fori_loop(0, NBLK, fill, 0)


def weights(panel, pattern, parts, extra):
    basis = panel.shape[0]
    layout = lane_layout(parts, extra, basis).T
    lanes = layout.shape[0]
    return pl.pallas_call(
        functools.partial(weights_kernel, sum(parts)),
        out_shape=jax.ShapeDtypeStruct((NBLK, 2 * lanes, 2 * basis), jnp.bfloat16),
        in_specs=[
            pl.BlockSpec(memory_space=pltpu.SMEM),
            pl.BlockSpec(memory_space=pltpu.VMEM),
            pl.BlockSpec(memory_space=pltpu.VMEM),
        ],
        out_specs=pl.BlockSpec(memory_space=pltpu.VMEM),
        compiler_params=pltpu.CompilerParams(vmem_limit_bytes=VMEM),
        cost_estimate=pl.CostEstimate(flops=2 * NBLK * 2 * lanes * basis * basis, bytes_accessed=2 * panel.nbytes, transcendentals=0),
        name="weights",
    )(pattern, jnp.asarray(layout), panel)


def contract_kernel(parts, extra, groups, per, me_ref, tables_hbm, got_hbm, *refs):
    more_hbm = refs[: PLANES if extra else 0]
    out_ref, tables, got, more, left, right, sems, more_sems = refs[len(more_hbm) :]
    count, _, basis = got.shape
    sources = count // NBLK
    height = right.shape[1] // basis * 8
    step = height // groups
    wide = count * 8

    def arrivals(block):
        here = pl.ds(block * sources, sources)
        return (
            pltpu.make_async_copy(tables_hbm.at[block], tables.at[block], sems.at[block, 0]),
            pltpu.make_async_copy(got_hbm.at[here], got.at[here], sems.at[block, 1]),
        )

    def more_arrival(away):
        level = lax.bitwise_xor(lax.div(me_ref[0] * PLANES, count), away)
        return pltpu.make_async_copy(more_hbm[away], more.at[level], more_sems.at[away])

    for block in range(NBLK):
        for copy in arrivals(block):
            copy.start()
        if extra and block == 0:
            for away in range(PLANES):
                more_arrival(away).start()
    for away in range(len(more_hbm)):
        more_arrival(away).wait()

    def unpack(block, _):
        for copy in arrivals(block):
            copy.wait()
        here = pl.ds(block * sources, sources)
        pieces, start = [], 0
        for index, piece in enumerate(with_extra(parts, extra)):
            shared = FULL // piece
            kept = groups // shared * step
            if index < len(parts):
                part = got[here, pl.ds(start, kept), :]
            else:
                part = more[lax.div(block, 2)]
            start += kept
            if shared > 1:
                lane = lax.broadcasted_iota(jnp.int32, part.shape, 2)
                window = basis // shared
                part = jnp.concatenate(
                    [
                        jnp.where((lane >= own * window) & (lane < (own + 1) * window), part, jnp.zeros_like(part))
                        for own in range(shared)
                    ],
                    axis=1,
                )
            pieces.append(part.reshape(sources * height, basis))
        both = jnp.concatenate(pieces + pieces, axis=1)
        turned = jnp.dot(both, tables[block], preferred_element_type=jnp.float32).reshape(sources, height, 2 * basis)
        rows = pl.ds(pl.multiple_of(block * (sources * 8), sources * 8), sources * 8)
        low_rows = pl.ds(pl.multiple_of(block * (sources * 8) + wide, sources * 8), sources * 8)
        for eight in range(height // 8):
            lanes = slice(eight * basis, (eight + 1) * basis)
            mine = turned[:, eight * 8 : eight * 8 + 8, :].reshape(sources * 8, 2 * basis)
            high = mine[:, :basis].astype(jnp.bfloat16)
            left[rows, lanes] = high
            left[low_rows, lanes] = (mine[:, :basis] - high.astype(jnp.float32)).astype(jnp.bfloat16)
            right[rows, lanes] = mine[:, basis:].astype(jnp.bfloat16)
        return 0

    lax.fori_loop(0, NBLK, unpack, 0)
    turns = right.shape[1] // DEPTH if right.shape[1] % DEPTH == 0 else 1
    depth = right.shape[1] // turns

    def multiply(turn, sums):
        lanes = pl.ds(pl.multiple_of(turn * depth, depth), depth)
        return sums + lax.dot_general(left[:, lanes], right[:, lanes], NT, preferred_element_type=jnp.float32)

    total = lax.fori_loop(0, turns, multiply, jnp.zeros((2 * wide, wide), jnp.float32))
    total = total[:wide] + total[wide:]
    row = lax.broadcasted_iota(jnp.int32, (wide, wide), 0) % 8 // per
    column = lax.broadcasted_iota(jnp.int32, (wide, wide), 1) % 8 // per
    total = jnp.where(row == column, total, 0.0)
    spot = lax.broadcasted_iota(jnp.int32, (basis, wide), 1)
    spot = spot // 8 * per + spot % per
    fold = jnp.where(spot == lax.broadcasted_iota(jnp.int32, (basis, wide), 0), 1.0, 0.0).astype(jnp.bfloat16)
    high, low = halves(total)
    total = jnp.dot(fold, high, preferred_element_type=jnp.float32) + jnp.dot(
        fold, low, preferred_element_type=jnp.float32
    )
    high, low = halves(total)
    total = lax.dot_general(high, fold, NT, preferred_element_type=jnp.float32) + lax.dot_general(
        low, fold, NT, preferred_element_type=jnp.float32
    )
    out_ref[...] = total + total.T


def contract(me, got, more, tables, parts, extra, groups, height, per):
    count, _, basis = got.shape
    deep = height // 8 * basis
    return pl.pallas_call(
        functools.partial(contract_kernel, parts, extra, groups, per),
        out_shape=jax.ShapeDtypeStruct((basis, basis), jnp.float32),
        in_specs=[pl.BlockSpec(memory_space=pltpu.SMEM)] + [pl.BlockSpec(memory_space=pl.ANY)] * (2 + len(more)),
        out_specs=pl.BlockSpec(memory_space=pltpu.VMEM),
        scratch_shapes=[
            pltpu.VMEM(tables.shape, jnp.bfloat16),
            pltpu.VMEM(got.shape, jnp.bfloat16),
            pltpu.VMEM((PLANES,) + (more[0].shape if extra else (8, basis)), jnp.bfloat16),
            pltpu.VMEM((count * 16, deep), jnp.bfloat16),
            pltpu.VMEM((count * 8, deep), jnp.bfloat16),
            pltpu.SemaphoreType.DMA((NBLK, 2)),
            pltpu.SemaphoreType.DMA((PLANES,)),
        ],
        compiler_params=pltpu.CompilerParams(vmem_limit_bytes=VMEM),
        name="contract",
    )(me, tables, got, *more)


def swap(rows, mask, count):
    return lax.ppermute(rows, "wide", [(i, i ^ mask) for i in range(count)]) if mask else rows


def widen(rows, bits, count):
    me, size = lax.axis_index("wide"), 2 ** len(bits)
    masks = [sum(bit for place, bit in enumerate(reversed(bits)) if turn >> place & 1) for turn in range(size)]
    got = [swap(rows, mask, count) for mask in masks]
    for place, bit in enumerate(reversed(bits)):
        low = me // bit % 2 == 0
        got = [jnp.where(low, got[turn], got[turn ^ 1 << place]) for turn in range(size)]
    return jnp.stack(got, axis=1).reshape((-1,) + rows.shape[1:])


def choose(pattern, plans):
    def kernel(pattern_ref, out_ref):
        alive = [surplus(pattern_ref, block, 0) for block in range(NBLK)]
        choice = jnp.int32(len(plans) - 1)
        for index, (direct, extra) in reversed(list(enumerate(plans[:-1]))):
            needed = jnp.int32(0)
            for level in range(PLANES):
                pair = jnp.maximum(alive[2 * level] - direct, 0) + jnp.maximum(alive[2 * level + 1] - direct, 0)
                needed = jnp.maximum(needed, pair)
            choice = jnp.where(needed <= extra, index, choice)
        out_ref[0] = choice

    return pl.pallas_call(
        kernel,
        out_shape=jax.ShapeDtypeStruct((1,), jnp.int32),
        in_specs=[pl.BlockSpec(memory_space=pltpu.SMEM)],
        out_specs=pl.BlockSpec(memory_space=pltpu.SMEM),
        name="choose",
    )(pattern)[0]


def share(parts, extra, groups, count, integrals, fitted, occupied, pattern):
    aux, per, basis = integrals.shape
    height = aux // count * per
    plane = count // PLANES
    me = lax.axis_index("wide").astype(jnp.int32).reshape(1)
    packed, *over = pack(
        integrals.reshape(count, height, basis), fitted.reshape(count, height, basis), me, pattern, parts, extra, groups
    )
    panel = occupied[None]
    bits = [1 << place for place in reversed(range(count.bit_length() - 1))]
    doubling = count & (count - 1) == 0
    if doubling:
        panel = widen(panel, bits[:2], count)
    packed, panel, over = lax.optimization_barrier((packed, panel, over))
    got = lax.all_to_all(packed, "wide", split_axis=0, concat_axis=0, tiled=True)
    more = []
    if extra:
        over = [swap(rows, apart, count) for apart, rows in enumerate(over)]
        sorted_rows = sort(jnp.stack(over), me, pattern, sum(parts), extra)
        more = [swap(sorted_rows[away], away * plane, count) for away in range(PLANES)]
    if doubling:
        panel = widen(panel, bits[2:], count)
    else:
        panel = lax.all_gather(panel, "wide", axis=0, tiled=True)
    tables = weights(panel.reshape(basis, -1), pattern, parts, extra)
    return contract(me, got, more, tables, parts, extra, groups, height, per)


def on_device(count, narrow, integrals, fitted, occupied, pattern):
    aux, per, basis = integrals.shape
    groups = next(g for g in (FULL, FULL // 2, 1) if aux // count * per % (16 * g) == 0)
    paired = groups == FULL and count & (count - 1) == 0
    plans = PLANS if paired else [(direct, 0) for direct in range(1, NBLK + 1) if parts_of(direct, groups)]
    branches = [functools.partial(share, parts_of(direct, groups), extra, groups, count) for direct, extra in plans]
    total = lax.switch(choose(pattern, plans), branches, integrals, fitted, occupied, pattern)
    strips = lax.all_to_all(total.reshape(count, per, basis), "wide", split_axis=0, concat_axis=0, tiled=True)
    strip = jnp.sum(strips.reshape(count, per, basis), axis=0)
    return lax.psum(strip, "narrow") if narrow > 1 else strip


def solution(mesh):
    in_specs = (P("narrow", "wide", None), P("narrow", "wide", None), P("wide", None), P())
    out_specs = P("wide", None)
    body = functools.partial(on_device, mesh.shape["wide"], mesh.shape["narrow"])
    return jax.shard_map(body, mesh=mesh, in_specs=in_specs, out_specs=out_specs, check_vma=False)
```

profile of v0, /device:TPU:0, one launch (start us, length us, event | category | flops | bytes accessed | tf_op | source)
XLA Modules:
  0.0 123.2 jit_solution(8979769333143946698)
XLA Ops:
  0.0 1.4 %choose.1 = s32[1]{0:T(128)} custom-call(s32[8,8]{1,0:T(8,128)} %pattern_ref.1), custom_call_target="tpu_custom_call" | custom-call | tf_op jit(solution)/shard_map/choose/pallas_call | solution.py:392
  2.0 109.8 %conditional.1 = (f32[128,128]{1,0:T(8,128)S(1)}) conditional(s32[]{:T(128)} %bitcast.167, (bf16[2048,4,128]{2,1,0:T(4,128)(2,1)}, bf16[2048,4,128]{2,1,0:T(4,128)(2,1)}, s32[8,8]{1,0:T(8,128)}, (), bf16[4,1024]{1,0:T(4,128)(2,1)}, /*index=5*/(), s32[3,128]{1,0:T(4,128)}) %tuple.33, (bf16[2048,4,128]{2,1,0:T(4,128)(2,1)}, ...), branch_computations={%region_0.1_spmd, %region_1.2_spmd, %region_2.3_spmd, %region_3.4_... | conditional | flops 1946763392 | bytes 36578504 | solution.py:435
  10.5 4.1 %collective-permute-start.81 = (bf16[1,4,1024]{2,1,0:T(4,128)(2,1)}, bf16[1,4,1024]{2,1,0:T(4,128)(2,1)S(1)}, u32[]{:S(2)}, u32[]{:S(2)}) collective-permute-start(bf16[1,4,1024]{2,1,0:T(4,128)(2,1)} %bitcast.365), channel_id=1, source_target_pairs={{0,16},{1,17},{2,18},{3,19},{4,20},{5,21},{6,22},{7,23},{8,24},{9,... | collective-permute-start | bytes 24584 | tf_op jit(solution)/shard_map/cond/branch_5_fun/ppermute | solution.py:367
  14.6 1.3 %collective-permute-start.82 = (bf16[1,4,1024]{2,1,0:T(4,128)(2,1)}, bf16[1,4,1024]{2,1,0:T(4,128)(2,1)S(1)}, u32[]{:S(2)}, u32[]{:S(2)}) collective-permute-start(bf16[1,4,1024]{2,1,0:T(4,128)(2,1)} %bitcast.366), channel_id=1, source_target_pairs={{0,24},{1,25},{2,26},{3,27},{4,28},{5,29},{6,30},{7,31},{8,16},{9,... | collective-permute-start | bytes 24584 | tf_op jit(solution)/shard_map/cond/branch_5_fun/ppermute | solution.py:367
  15.9 0.2 collective-permute-start.80
  16.2 6.3 %pack.12 = (bf16[32,320,128]{2,1,0:T(8,128)(2,1)}, bf16[4,128,128]{2,1,0:T(8,128)(2,1)}, bf16[4,128,128]{2,1,0:T(8,128)(2,1)}, bf16[4,128,128]{2,1,0:T(8,128)(2,...) custom-call(s32[1]{0:T(128)} %bitcast.121.me_ref, ...), custom_call_target="tpu_custom_call" | custom-call | flops 1610612736 | bytes 7864320 | tf_op jit(solution)/shard_map/cond/branch_5_fun/pack/pallas_call | solution.py:146
  22.5 0.0 collective-permute-done.81
  22.7 5.7 %all-to-all-start.5 = ((bf16[32,320,128]{2,1,0:T(8,128)(2,1)}), bf16[32,320,128]{2,1,0:T(8,128)(2,1)}, u32[]{:S(2)}, u32[]{:S(2)}) async-start(bf16[32,320,128]{2,1,0:T(8,128)(2,1)} %get-tuple-element.215), calls=%async_computation.5 | async-start | bytes 5242880 | tf_op jit(solution)/shard_map/cond/branch_5_fun/all_to_all | solution.py:415
  28.4 0.0 copy-start.5
  28.4 0.0 copy-start.33
  28.4 2.1 %collective-permute-start.89 = (bf16[4,4,1024]{2,1,0:T(4,128)(2,1)S(1)}, bf16[4,4,1024]{2,1,0:T(4,128)(2,1)S(1)}, u32[]{:S(2)}, u32[]{:S(2)}) collective-permute-start(bf16[4,4,1024]{2,1,0:T(4,128)(2,1)S(1)} %maximum_bitcast_fusion.5), channel_id=1, source_target_pairs={{0,7},{1,6},{2,5},{3,4},{4,3},{5,2},{6,1},{7,0},{8,15},{9,14},{10,... | collective-permute-start | bytes 98312 | tf_op jit(solution)/shard_map/cond/branch_5_fun/ppermute | solution.py:367
  30.5 0.4 collective-permute-start.88
  30.8 1.4 %collective-permute-start.87 = (bf16[4,4,1024]{2,1,0:T(4,128)(2,1)S(1)}, bf16[4,4,1024]{2,1,0:T(4,128)(2,1)S(1)}, u32[]{:S(2)}, u32[]{:S(2)}) collective-permute-start(bf16[4,4,1024]{2,1,0:T(4,128)(2,1)S(1)} %maximum_bitcast_fusion.5), channel_id=1, source_target_pairs={{0,5},{1,4},{2,7},{3,6},{4,1},{5,0},{6,3},{7,2},{8,13},{9,12},{10,... | collective-permute-start | bytes 98312 | tf_op jit(solution)/shard_map/cond/branch_5_fun/ppermute | solution.py:367
  32.2 0.7 collective-permute-start.86
  32.8 1.1 collective-permute-start.85
  34.0 12.0 %collective-permute-done.89 = bf16[4,4,1024]{2,1,0:T(4,128)(2,1)S(1)} collective-permute-done((bf16[4,4,1024]{2,1,0:T(4,128)(2,1)S(1)}, bf16[4,4,1024]{2,1,0:T(4,128)(2,1)S(1)}, u32[]{:S(2)}, u32[]{:S(2)}) %collective-permute-start.89) | collective-permute-done | bytes 32800 | tf_op jit(solution)/shard_map/cond/branch_5_fun/ppermute | solution.py:367
  46.0 3.2 %collective-permute-start.84 = (bf16[4,4,1024]{2,1,0:T(4,128)(2,1)S(1)}, bf16[4,4,1024]{2,1,0:T(4,128)(2,1)S(1)}, u32[]{:S(2)}, u32[]{:S(2)}) collective-permute-start(bf16[4,4,1024]{2,1,0:T(4,128)(2,1)S(1)} %maximum_bitcast_fusion.5), channel_id=1, source_target_pairs={{0,2},{1,3},{2,0},{3,1},{4,6},{5,7},{6,4},{7,5},{8,10},{9,11},{10,... | collective-permute-start | bytes 98312 | tf_op jit(solution)/shard_map/cond/branch_5_fun/ppermute | solution.py:367
  49.2 1.4 %collective-permute-start.83 = (bf16[4,4,1024]{2,1,0:T(4,128)(2,1)S(1)}, bf16[4,4,1024]{2,1,0:T(4,128)(2,1)S(1)}, u32[]{:S(2)}, u32[]{:S(2)}) collective-permute-start(bf16[4,4,1024]{2,1,0:T(4,128)(2,1)S(1)} %maximum_bitcast_fusion.5), channel_id=1, source_target_pairs={{0,1},{1,0},{2,3},{3,2},{4,5},{5,4},{6,7},{7,6},{8,9},{9,8},{10,11... | collective-permute-start | bytes 98312 | tf_op jit(solution)/shard_map/cond/branch_5_fun/ppermute | solution.py:367
  50.6 0.0 collective-permute-done.87
  50.6 0.1 collective-permute-start.90
  50.7 2.4 %collective-permute-start.91 = (bf16[4,128,128]{2,1,0:T(8,128)(2,1)S(1)}, bf16[4,128,128]{2,1,0:T(8,128)(2,1)S(1)}, u32[]{:S(2)}, u32[]{:S(2)}) collective-permute-start(bf16[4,128,128]{2,1,0:T(8,128)(2,1)S(1)} %copy-done.45), channel_id=1, source_target_pairs={{0,2},{1,3},{2,0},{3,1},{4,6},{5,7},{6,4},{7,5},{8,10},{9,11},{10,... | collective-permute-start | bytes 393224 | tf_op jit(solution)/shard_map/cond/branch_5_fun/ppermute | solution.py:367
  53.1 0.0 collective-permute-done.85
  53.1 0.0 collective-permute-done.84
  53.2 1.3 %collective-permute-start.93 = (bf16[4,128,128]{2,1,0:T(8,128)(2,1)S(1)}, bf16[4,128,128]{2,1,0:T(8,128)(2,1)S(1)}, u32[]{:S(2)}, u32[]{:S(2)}) collective-permute-start(bf16[4,128,128]{2,1,0:T(8,128)(2,1)S(1)} %copy-done.41), channel_id=1, source_target_pairs={{0,4},{1,5},{2,6},{3,7},{4,0},{5,1},{6,2},{7,3},{8,12},{9,13},{10,... | collective-permute-start | bytes 393224 | tf_op jit(solution)/shard_map/cond/branch_5_fun/ppermute | solution.py:367
  54.5 0.0 collective-permute-done.83
  54.5 0.4 collective-permute-start.94
  54.9 0.1 constant_dynamic-update-slice_fusion.31
  55.0 0.1 constant_dynamic-update-slice_fusion.30
  55.2 0.1 constant_dynamic-update-slice_fusion.28
  55.3 0.1 constant_dynamic-update-slice_fusion.26
  55.4 0.0 collective-permute-done.90
  55.4 1.6 %collective-permute-start.95 = (bf16[4,128,128]{2,1,0:T(8,128)(2,1)S(1)}, bf16[4,128,128]{2,1,0:T(8,128)(2,1)S(1)}, u32[]{:S(2)}, u32[]{:S(2)}) collective-permute-start(bf16[4,128,128]{2,1,0:T(8,128)(2,1)S(1)} %copy-done.37), channel_id=1, source_target_pairs={{0,6},{1,7},{2,4},{3,5},{4,2},{5,3},{6,0},{7,1},{8,14},{9,15},{10,... | collective-permute-start | bytes 393224 | tf_op jit(solution)/shard_map/cond/branch_5_fun/ppermute | solution.py:367
  57.0 7.9 %collective-permute-done.91 = bf16[4,128,128]{2,1,0:T(8,128)(2,1)S(1)} collective-permute-done((bf16[4,128,128]{2,1,0:T(8,128)(2,1)S(1)}, bf16[4,128,128]{2,1,0:T(8,128)(2,1)S(1)}, u32[]{:S(2)}, u32[]{:S(2)}) %collective-permute-start.91) | collective-permute-done | bytes 131104 | tf_op jit(solution)/shard_map/cond/branch_5_fun/ppermute | solution.py:367
  65.0 2.3 %collective-permute-done.92 = bf16[4,128,128]{2,1,0:T(8,128)(2,1)S(1)} collective-permute-done((bf16[4,128,128]{2,1,0:T(8,128)(2,1)S(1)}, bf16[4,128,128]{2,1,0:T(8,128)(2,1)S(1)}, u32[]{:S(2)}, u32[]{:S(2)}) %collective-permute-start.92) | collective-permute-done | bytes 131104 | tf_op jit(solution)/shard_map/cond/branch_5_fun/ppermute | solution.py:367
  67.3 5.3 %collective-permute-done.94 = bf16[4,128,128]{2,1,0:T(8,128)(2,1)S(1)} collective-permute-done((bf16[4,128,128]{2,1,0:T(8,128)(2,1)S(1)}, bf16[4,128,128]{2,1,0:T(8,128)(2,1)S(1)}, u32[]{:S(2)}, u32[]{:S(2)}) %collective-permute-start.94) | collective-permute-done | bytes 131104 | tf_op jit(solution)/shard_map/cond/branch_5_fun/ppermute | solution.py:367
  72.8 1.5 %sort.7 = bf16[4,4,128,128]{3,2,1,0:T(8,128)(2,1)S(1)} custom-call(s32[1]{0:T(128)} %bitcast.121.me_ref, s32[8,8]{1,0:T(8,128)S(1)} %copy-done.5, s32[3,128]{1,0:T(4,128)S(1)} %copy-done.33, bf16[8,4,128,128]{3,2,1,0:T(8,128)(2,1)S(1)} %bitcast_dynamic-update-slice_fusion.40.over_ref), custom_call_target="tpu_custom_call" | custom-call | flops 134217728 | bytes 2097152 | tf_op jit(solution)/shard_map/cond/branch_5_fun/sort/pallas_call | solution.py:197
  74.3 0.7 slice_bitcast_fusion.12
  75.0 5.1 %collective-permute-start.99 = (bf16[4,128,128]{2,1,0:T(8,128)(2,1)S(1)}, bf16[4,128,128]{2,1,0:T(8,128)(2,1)S(1)}, u32[]{:S(2)}, u32[]{:S(2)}) collective-permute-start(bf16[4,128,128]{2,1,0:T(8,128)(2,1)S(1)} %get-tuple-element.363), channel_id=1, source_target_pairs={{0,24},{1,25},{2,26},{3,27},{4,28},{5,29},{6,30},{7,31},{8,16},{9,... | collective-permute-start | bytes 393224 | tf_op jit(solution)/shard_map/cond/branch_5_fun/ppermute | solution.py:367
  80.1 1.3 %collective-permute-start.98 = (bf16[4,128,128]{2,1,0:T(8,128)(2,1)S(1)}, bf16[4,128,128]{2,1,0:T(8,128)(2,1)S(1)}, u32[]{:S(2)}, u32[]{:S(2)}) collective-permute-start(bf16[4,128,128]{2,1,0:T(8,128)(2,1)S(1)} %get-tuple-element.364), channel_id=1, source_target_pairs={{0,16},{1,17},{2,18},{3,19},{4,20},{5,21},{6,22},{7,23},{8,24},{9,... | collective-permute-start | bytes 393224 | tf_op jit(solution)/shard_map/cond/branch_5_fun/ppermute | solution.py:367
  81.4 0.1 copy.42
  81.5 0.8 reshape.104.panel_ref
  82.3 10.1 %weights.12.tables_hbm = bf16[8,768,256]{2,1,0:T(8,128)(2,1)} custom-call(s32[8,8]{1,0:T(8,128)S(1)} %copy-done.5, s32[384,3]{1,0:T(8,128)} %constant.624.clone.1.layout_ref, bf16[128,1024]{1,0:T(8,128)(2,1)} %reshape.104.panel_ref), custom_call_target="tpu_custom_call" | custom-call | flops 201326592 | bytes 524288 | tf_op jit(solution)/shard_map/cond/branch_5_fun/weights/pallas_call | solution.py:236
  92.4 7.6 %collective-permute-done.98.refs_2_ = bf16[4,128,128]{2,1,0:T(8,128)(2,1)S(1)} collective-permute-done((bf16[4,128,128]{2,1,0:T(8,128)(2,1)S(1)}, bf16[4,128,128]{2,1,0:T(8,128)(2,1)S(1)}, u32[]{:S(2)}, u32[]{:S(2)}) %collective-permute-start.98) | collective-permute-done | bytes 131104 | tf_op jit(solution)/shard_map/cond/branch_5_fun/ppermute | solution.py:367
  100.0 0.6 copy-done.17
  100.6 0.0 copy-done.19
  100.7 9.8 %contract.12 = f32[128,128]{1,0:T(8,128)S(1)} custom-call(s32[1]{0:T(128)} %bitcast.121.me_ref, bf16[8,768,256]{2,1,0:T(8,128)(2,1)} %weights.12.tables_hbm, bf16[32,320,128]{2,1,0:T(8,128)(2,1)} %all-to-all-done.5.got_hbm, bf16[4,128,128]{2,1,0:T(8,128)(2,1)} %get-tuple-element.366.refs_0_, bf16[4,128,128]{2,1,0:T(8,128)(2,1)} %copy-done.19, ...), custom_call_target="tpu_custom_call" | custom-call | tf_op jit(solution)/shard_map/cond/branch_5_fun/contract/pallas_call | solution.py:347
  111.8 10.5 %all_to_all.33 = f32[32,4,128]{2,1,0:T(4,128)S(1)} all-to-all(f32[32,4,128]{2,1,0:T(4,128)S(1)} %bitcast.371), channel_id=1, replica_groups=mesh['wide'=32,'narrow'=1] {'wide'}, dimensions={0} | all-to-all | bytes 131072 | tf_op jit(solution)/shard_map/all_to_all | solution.py:436
  122.3 0.6 reduce_sum.9
  (51 shorter events, 0.5 us)
Async XLA Ops:
  10.5 12.0 %collective-permute-start.81 = (bf16[1,4,1024]{2,1,0:T(4,128)(2,1)}, bf16[1,4,1024]{2,1,0:T(4,128)(2,1)S(1)}, u32[]{:S(2)}, u32[]{:S(2)}) collective-permute-start(bf16[1,4,1024]{2,1,0:T(4,128)(2,1)} %bitcast.365), channel_id=1, source_target_pairs={{0,16},{1,17},{2,18},{3,19},{4,20},{5,21},{6,22},{7,23},{8,24},{9,... | collective-permute-start | bytes 24584 | tf_op jit(solution)/shard_map/cond/branch_5_fun/ppermute | solution.py:367
  14.6 7.9 %collective-permute-start.82 = (bf16[1,4,1024]{2,1,0:T(4,128)(2,1)}, bf16[1,4,1024]{2,1,0:T(4,128)(2,1)S(1)}, u32[]{:S(2)}, u32[]{:S(2)}) collective-permute-start(bf16[1,4,1024]{2,1,0:T(4,128)(2,1)} %bitcast.366), channel_id=1, source_target_pairs={{0,24},{1,25},{2,26},{3,27},{4,28},{5,29},{6,30},{7,31},{8,16},{9,... | collective-permute-start | bytes 24584 | tf_op jit(solution)/shard_map/cond/branch_5_fun/ppermute | solution.py:367
  15.9 6.6 %collective-permute-start.80 = (bf16[1,4,1024]{2,1,0:T(4,128)(2,1)}, bf16[1,4,1024]{2,1,0:T(4,128)(2,1)S(1)}, u32[]{:S(2)}, u32[]{:S(2)}) collective-permute-start(bf16[1,4,1024]{2,1,0:T(4,128)(2,1)} %bitcast.367), channel_id=1, source_target_pairs={{0,8},{1,9},{2,10},{3,11},{4,12},{5,13},{6,14},{7,15},{8,0},{9,1},... | collective-permute-start | bytes 24584 | tf_op jit(solution)/shard_map/cond/branch_5_fun/ppermute | solution.py:367
  16.2 6.4 %copy-start.12 = (bf16[4,1024]{1,0:T(4,128)(2,1)S(1)}, bf16[4,1024]{1,0:T(4,128)(2,1)}, u32[]{:S(2)}) copy-start(bf16[4,1024]{1,0:T(4,128)(2,1)} %get-tuple-element.205) | copy-start | bytes 24580 | tf_op jit(solution)/shard_map/cond
  22.6 28.0 %copy-start.21 = (bf16[4,128,128]{2,1,0:T(8,128)(2,1)S(1)}, bf16[4,128,128]{2,1,0:T(8,128)(2,1)}, u32[]{:S(2)}) copy-start(bf16[4,128,128]{2,1,0:T(8,128)(2,1)} %get-tuple-element.217) | copy-start | bytes 393220 | tf_op jit(solution)/shard_map/cond
  22.6 28.0 %copy-start.47 = (bf16[4,128,128]{2,1,0:T(8,128)(2,1)S(1)}, bf16[4,128,128]{2,1,0:T(8,128)(2,1)}, u32[]{:S(2)}) copy-start(bf16[4,128,128]{2,1,0:T(8,128)(2,1)} %get-tuple-element.218) | copy-start | bytes 393220 | tf_op jit(solution)/shard_map/cond
  22.6 28.1 %copy-start.45 = (bf16[4,128,128]{2,1,0:T(8,128)(2,1)S(1)}, bf16[4,128,128]{2,1,0:T(8,128)(2,1)}, u32[]{:S(2)}) copy-start(bf16[4,128,128]{2,1,0:T(8,128)(2,1)} %get-tuple-element.219) | copy-start | bytes 393220 | tf_op jit(solution)/shard_map/cond
  22.6 30.5 %copy-start.43 = (bf16[4,128,128]{2,1,0:T(8,128)(2,1)S(1)}, bf16[4,128,128]{2,1,0:T(8,128)(2,1)}, u32[]{:S(2)}) copy-start(bf16[4,128,128]{2,1,0:T(8,128)(2,1)} %get-tuple-element.220) | copy-start | bytes 393220 | tf_op jit(solution)/shard_map/cond
  22.7 30.5 %copy-start.41 = (bf16[4,128,128]{2,1,0:T(8,128)(2,1)S(1)}, bf16[4,128,128]{2,1,0:T(8,128)(2,1)}, u32[]{:S(2)}) copy-start(bf16[4,128,128]{2,1,0:T(8,128)(2,1)} %get-tuple-element.221) | copy-start | bytes 393220 | tf_op jit(solution)/shard_map/cond
  22.7 31.8 %copy-start.39 = (bf16[4,128,128]{2,1,0:T(8,128)(2,1)S(1)}, bf16[4,128,128]{2,1,0:T(8,128)(2,1)}, u32[]{:S(2)}) copy-start(bf16[4,128,128]{2,1,0:T(8,128)(2,1)} %get-tuple-element.222) | copy-start | bytes 393220 | tf_op jit(solution)/shard_map/cond
  22.7 32.7 %copy-start.37 = (bf16[4,128,128]{2,1,0:T(8,128)(2,1)S(1)}, bf16[4,128,128]{2,1,0:T(8,128)(2,1)}, u32[]{:S(2)}) copy-start(bf16[4,128,128]{2,1,0:T(8,128)(2,1)} %get-tuple-element.223) | copy-start | bytes 393220 | tf_op jit(solution)/shard_map/cond
  22.7 42.3 %copy-start.35 = (bf16[4,128,128]{2,1,0:T(8,128)(2,1)S(1)}, bf16[4,128,128]{2,1,0:T(8,128)(2,1)}, u32[]{:S(2)}) copy-start(bf16[4,128,128]{2,1,0:T(8,128)(2,1)} %get-tuple-element.224) | copy-start | bytes 393220 | tf_op jit(solution)/shard_map/cond
  22.7 77.3 %all-to-all-start.5 = ((bf16[32,320,128]{2,1,0:T(8,128)(2,1)}), bf16[32,320,128]{2,1,0:T(8,128)(2,1)}, u32[]{:S(2)}, u32[]{:S(2)}) async-start(bf16[32,320,128]{2,1,0:T(8,128)(2,1)} %get-tuple-element.215), calls=%async_computation.5 | async-start | bytes 5242880 | tf_op jit(solution)/shard_map/cond/branch_5_fun/all_to_all | solution.py:415
  28.4 44.4 %copy-start.5 = (s32[8,8]{1,0:T(8,128)S(1)}, s32[8,8]{1,0:T(8,128)}, u32[]{:S(2)}) copy-start(s32[8,8]{1,0:T(8,128)} %get-tuple-element.199.pattern_ref) | copy-start | bytes 772 | tf_op jit(solution)/shard_map/cond
  28.4 44.4 %copy-start.33 = (s32[3,128]{1,0:T(4,128)S(1)}, s32[3,128]{1,0:T(4,128)}, u32[]{:S(2)}) copy-start(s32[3,128]{1,0:T(4,128)} %get-tuple-element.216.slot_ref) | copy-start | bytes 4612 | tf_op jit(solution)/shard_map/cond
  28.4 17.6 %collective-permute-start.89 = (bf16[4,4,1024]{2,1,0:T(4,128)(2,1)S(1)}, bf16[4,4,1024]{2,1,0:T(4,128)(2,1)S(1)}, u32[]{:S(2)}, u32[]{:S(2)}) collective-permute-start(bf16[4,4,1024]{2,1,0:T(4,128)(2,1)S(1)} %maximum_bitcast_fusion.5), channel_id=1, source_target_pairs={{0,7},{1,6},{2,5},{3,4},{4,3},{5,2},{6,1},{7,0},{8,15},{9,14},{10,... | collective-permute-start | bytes 98312 | tf_op jit(solution)/shard_map/cond/branch_5_fun/ppermute | solution.py:367
  30.5 18.7 %collective-permute-start.88 = (bf16[4,4,1024]{2,1,0:T(4,128)(2,1)S(1)}, bf16[4,4,1024]{2,1,0:T(4,128)(2,1)S(1)}, u32[]{:S(2)}, u32[]{:S(2)}) collective-permute-start(bf16[4,4,1024]{2,1,0:T(4,128)(2,1)S(1)} %maximum_bitcast_fusion.5), channel_id=1, source_target_pairs={{0,6},{1,7},{2,4},{3,5},{4,2},{5,3},{6,0},{7,1},{8,14},{9,15},{10,... | collective-permute-start | bytes 98312 | tf_op jit(solution)/shard_map/cond/branch_5_fun/ppermute | solution.py:367
  30.8 19.8 %collective-permute-start.87 = (bf16[4,4,1024]{2,1,0:T(4,128)(2,1)S(1)}, bf16[4,4,1024]{2,1,0:T(4,128)(2,1)S(1)}, u32[]{:S(2)}, u32[]{:S(2)}) collective-permute-start(bf16[4,4,1024]{2,1,0:T(4,128)(2,1)S(1)} %maximum_bitcast_fusion.5), channel_id=1, source_target_pairs={{0,5},{1,4},{2,7},{3,6},{4,1},{5,0},{6,3},{7,2},{8,13},{9,12},{10,... | collective-permute-start | bytes 98312 | tf_op jit(solution)/shard_map/cond/branch_5_fun/ppermute | solution.py:367
  32.2 18.5 %collective-permute-start.86 = (bf16[4,4,1024]{2,1,0:T(4,128)(2,1)S(1)}, bf16[4,4,1024]{2,1,0:T(4,128)(2,1)S(1)}, u32[]{:S(2)}, u32[]{:S(2)}) collective-permute-start(bf16[4,4,1024]{2,1,0:T(4,128)(2,1)S(1)} %maximum_bitcast_fusion.5), channel_id=1, source_target_pairs={{0,4},{1,5},{2,6},{3,7},{4,0},{5,1},{6,2},{7,3},{8,12},{9,13},{10,... | collective-permute-start | bytes 98312 | tf_op jit(solution)/shard_map/cond/branch_5_fun/ppermute | solution.py:367
  32.8 20.3 %collective-permute-start.85 = (bf16[4,4,1024]{2,1,0:T(4,128)(2,1)S(1)}, bf16[4,4,1024]{2,1,0:T(4,128)(2,1)S(1)}, u32[]{:S(2)}, u32[]{:S(2)}) collective-permute-start(bf16[4,4,1024]{2,1,0:T(4,128)(2,1)S(1)} %maximum_bitcast_fusion.5), channel_id=1, source_target_pairs={{0,3},{1,2},{2,1},{3,0},{4,7},{5,6},{6,5},{7,4},{8,11},{9,10},{10,... | collective-permute-start | bytes 98312 | tf_op jit(solution)/shard_map/cond/branch_5_fun/ppermute | solution.py:367
  46.0 7.2 %collective-permute-start.84 = (bf16[4,4,1024]{2,1,0:T(4,128)(2,1)S(1)}, bf16[4,4,1024]{2,1,0:T(4,128)(2,1)S(1)}, u32[]{:S(2)}, u32[]{:S(2)}) collective-permute-start(bf16[4,4,1024]{2,1,0:T(4,128)(2,1)S(1)} %maximum_bitcast_fusion.5), channel_id=1, source_target_pairs={{0,2},{1,3},{2,0},{3,1},{4,6},{5,7},{6,4},{7,5},{8,10},{9,11},{10,... | collective-permute-start | bytes 98312 | tf_op jit(solution)/shard_map/cond/branch_5_fun/ppermute | solution.py:367
  49.2 5.3 %collective-permute-start.83 = (bf16[4,4,1024]{2,1,0:T(4,128)(2,1)S(1)}, bf16[4,4,1024]{2,1,0:T(4,128)(2,1)S(1)}, u32[]{:S(2)}, u32[]{:S(2)}) collective-permute-start(bf16[4,4,1024]{2,1,0:T(4,128)(2,1)S(1)} %maximum_bitcast_fusion.5), channel_id=1, source_target_pairs={{0,1},{1,0},{2,3},{3,2},{4,5},{5,4},{6,7},{7,6},{8,9},{9,8},{10,11... | collective-permute-start | bytes 98312 | tf_op jit(solution)/shard_map/cond/branch_5_fun/ppermute | solution.py:367
  50.6 4.8 %collective-permute-start.90 = (bf16[4,128,128]{2,1,0:T(8,128)(2,1)S(1)}, bf16[4,128,128]{2,1,0:T(8,128)(2,1)S(1)}, u32[]{:S(2)}, u32[]{:S(2)}) collective-permute-start(bf16[4,128,128]{2,1,0:T(8,128)(2,1)S(1)} %copy-done.47), channel_id=1, source_target_pairs={{0,1},{1,0},{2,3},{3,2},{4,5},{5,4},{6,7},{7,6},{8,9},{9,8},{10,11... | collective-permute-start | bytes 393224 | tf_op jit(solution)/shard_map/cond/branch_5_fun/ppermute | solution.py:367
  50.7 14.2 %collective-permute-start.91 = (bf16[4,128,128]{2,1,0:T(8,128)(2,1)S(1)}, bf16[4,128,128]{2,1,0:T(8,128)(2,1)S(1)}, u32[]{:S(2)}, u32[]{:S(2)}) collective-permute-start(bf16[4,128,128]{2,1,0:T(8,128)(2,1)S(1)} %copy-done.45), channel_id=1, source_target_pairs={{0,2},{1,3},{2,0},{3,1},{4,6},{5,7},{6,4},{7,5},{8,10},{9,11},{10,... | collective-permute-start | bytes 393224 | tf_op jit(solution)/shard_map/cond/branch_5_fun/ppermute | solution.py:367
  53.1 14.1 %collective-permute-start.92 = (bf16[4,128,128]{2,1,0:T(8,128)(2,1)S(1)}, bf16[4,128,128]{2,1,0:T(8,128)(2,1)S(1)}, u32[]{:S(2)}, u32[]{:S(2)}) collective-permute-start(bf16[4,128,128]{2,1,0:T(8,128)(2,1)S(1)} %copy-done.43), channel_id=1, source_target_pairs={{0,3},{1,2},{2,1},{3,0},{4,7},{5,6},{6,5},{7,4},{8,11},{9,10},{10,... | collective-permute-start | bytes 393224 | tf_op jit(solution)/shard_map/cond/branch_5_fun/ppermute | solution.py:367
  53.2 14.1 %collective-permute-start.93 = (bf16[4,128,128]{2,1,0:T(8,128)(2,1)S(1)}, bf16[4,128,128]{2,1,0:T(8,128)(2,1)S(1)}, u32[]{:S(2)}, u32[]{:S(2)}) collective-permute-start(bf16[4,128,128]{2,1,0:T(8,128)(2,1)S(1)} %copy-done.41), channel_id=1, source_target_pairs={{0,4},{1,5},{2,6},{3,7},{4,0},{5,1},{6,2},{7,3},{8,12},{9,13},{10,... | collective-permute-start | bytes 393224 | tf_op jit(solution)/shard_map/cond/branch_5_fun/ppermute | solution.py:367
  54.5 18.1 %collective-permute-start.94 = (bf16[4,128,128]{2,1,0:T(8,128)(2,1)S(1)}, bf16[4,128,128]{2,1,0:T(8,128)(2,1)S(1)}, u32[]{:S(2)}, u32[]{:S(2)}) collective-permute-start(bf16[4,128,128]{2,1,0:T(8,128)(2,1)S(1)} %copy-done.39), channel_id=1, source_target_pairs={{0,5},{1,4},{2,7},{3,6},{4,1},{5,0},{6,3},{7,2},{8,13},{9,12},{10,... | collective-permute-start | bytes 393224 | tf_op jit(solution)/shard_map/cond/branch_5_fun/ppermute | solution.py:367
  55.4 17.3 %collective-permute-start.95 = (bf16[4,128,128]{2,1,0:T(8,128)(2,1)S(1)}, bf16[4,128,128]{2,1,0:T(8,128)(2,1)S(1)}, u32[]{:S(2)}, u32[]{:S(2)}) collective-permute-start(bf16[4,128,128]{2,1,0:T(8,128)(2,1)S(1)} %copy-done.37), channel_id=1, source_target_pairs={{0,6},{1,7},{2,4},{3,5},{4,2},{5,3},{6,0},{7,1},{8,14},{9,15},{10,... | collective-permute-start | bytes 393224 | tf_op jit(solution)/shard_map/cond/branch_5_fun/ppermute | solution.py:367
  64.9 7.8 %collective-permute-start.96 = (bf16[4,128,128]{2,1,0:T(8,128)(2,1)S(1)}, bf16[4,128,128]{2,1,0:T(8,128)(2,1)S(1)}, u32[]{:S(2)}, u32[]{:S(2)}) collective-permute-start(bf16[4,128,128]{2,1,0:T(8,128)(2,1)S(1)} %copy-done.35), channel_id=1, source_target_pairs={{0,7},{1,6},{2,5},{3,4},{4,3},{5,2},{6,1},{7,0},{8,15},{9,14},{10,... | collective-permute-start | bytes 393224 | tf_op jit(solution)/shard_map/cond/branch_5_fun/ppermute | solution.py:367
  75.0 17.4 %collective-permute-start.99 = (bf16[4,128,128]{2,1,0:T(8,128)(2,1)S(1)}, bf16[4,128,128]{2,1,0:T(8,128)(2,1)S(1)}, u32[]{:S(2)}, u32[]{:S(2)}) collective-permute-start(bf16[4,128,128]{2,1,0:T(8,128)(2,1)S(1)} %get-tuple-element.363), channel_id=1, source_target_pairs={{0,24},{1,25},{2,26},{3,27},{4,28},{5,29},{6,30},{7,31},{8,16},{9,... | collective-permute-start | bytes 393224 | tf_op jit(solution)/shard_map/cond/branch_5_fun/ppermute | solution.py:367
  80.1 19.9 %collective-permute-start.98 = (bf16[4,128,128]{2,1,0:T(8,128)(2,1)S(1)}, bf16[4,128,128]{2,1,0:T(8,128)(2,1)S(1)}, u32[]{:S(2)}, u32[]{:S(2)}) collective-permute-start(bf16[4,128,128]{2,1,0:T(8,128)(2,1)S(1)} %get-tuple-element.364), channel_id=1, source_target_pairs={{0,16},{1,17},{2,18},{3,19},{4,20},{5,21},{6,22},{7,23},{8,24},{9,... | collective-permute-start | bytes 393224 | tf_op jit(solution)/shard_map/cond/branch_5_fun/ppermute | solution.py:367
  81.3 18.7 %collective-permute-start.97 = (bf16[4,128,128]{2,1,0:T(8,128)(2,1)S(1)}, bf16[4,128,128]{2,1,0:T(8,128)(2,1)S(1)}, u32[]{:S(2)}, u32[]{:S(2)}) collective-permute-start(bf16[4,128,128]{2,1,0:T(8,128)(2,1)S(1)} %get-tuple-element.365), channel_id=1, source_target_pairs={{0,8},{1,9},{2,10},{3,11},{4,12},{5,13},{6,14},{7,15},{8,0},{9,1},... | collective-permute-start | bytes 393224 | tf_op jit(solution)/shard_map/cond/branch_5_fun/ppermute | solution.py:367
  92.4 7.6 %copy-start.15 = (bf16[4,128,128]{2,1,0:T(8,128)(2,1)}, bf16[4,128,128]{2,1,0:T(8,128)(2,1)S(1)}, u32[]{:S(2)}) copy-start(bf16[4,128,128]{2,1,0:T(8,128)(2,1)S(1)} %collective-permute-done.99.refs_3_) | copy-start | bytes 393220 | tf_op jit(solution)/shard_map/cond
  100.0 0.7 copy-start.17
  100.0 0.7 copy-start.19
where the time goes:
time: 122 us; the launch traced here: 123 us
  waiting for transfers between devices  35.2 us (29%)
  starting transfers between devices  33.7 us (28%)
  Pallas kernels  29 us (24%)
  blocking collectives  10.5 us (9%)
  loops' own time  10.2 us (8%)
  local copies, waits for them, and re-layouts  2.43 us (2%)
    ppermute x20, waiting for transfers between devices, swap(): lax.ppermute(rows, 'wide', [(i, i ^ mask) for i in range(count)])  35.2 us
    ppermute x20, starting transfers between devices, swap(): lax.ppermute(rows, 'wide', [(i, i ^ mask) for i in range(count)])  28.1 us
    all_to_all x1, blocking collectives, on_device(): lax.all_to_all(total.reshape(count, per, basis), 'wide', split_axis=0, co...  10.5 us
    another operation x1, loops' own time, on_device(): lax.switch(choose(pattern, plans), branches, integrals, fitted, occupied,...  10.2 us
    pallas_call x1, Pallas kernels, weights(): pl.pallas_call(functools.partial(weights_kernel, sum(parts)), out_shape=j...  10.1 us
    pallas_call x1, Pallas kernels, contract(): pl.pallas_call(functools.partial(contract_kernel, parts, extra, groups, p...  9.79 us
    pallas_call x1, Pallas kernels, pack(): pl.pallas_call(functools.partial(pack_kernel, parts, extra, groups), out_...  6.28 us
    all_to_all x1, starting transfers between devices, share(): lax.all_to_all(packed, 'wide', split_axis=0, concat_axis=0, tiled=True)  5.66 us
  transfers between devices with their start and end apart: 21, of which 5 were waited for; matrix products, arithmetic and copies ran while one was open for 2% of the time, Pallas kernels for 15%

commit v1 on v0

--- a/solution.py
+++ b/solution.py
@@ -15,7 +15,7 @@
 SORT_VMEM = 24 * 2**20
 NT = (((1,), (1,)), ((), ()))
 PLANES = NBLK // 2
-PLANS = ((4, 1), (5, 0), (4, 2), (5, 1), (6, 0), (5, 2), (8, 0))
+PLANS = ((4, 1), (5, 0), (4, 2), (6, 0), (5, 2), (8, 0))
 
 
 def parts_of(cap, groups):

time: 122 us -> 114 us (0.934); the launches traced: 123 us -> 114 us
  loops' own time: 10.2 us -> 0.99 us
    another operation x1, loops' own time: 10.2 us -> 0.99 us  [on_device(): lax.switch(choose(pattern, plans), branches, integrals, fitted, occupied,...]
  transfers between devices with their start and end apart: 21 -> 21, of which waited for: 5 -> 5; matrix products, arithmetic and copies ran while one was open for 2% -> 2% of each run, Pallas kernels for 15% -> 16%
where the time goes in v1:
time: 114 us
  waiting for transfers between devices  35.3 us (31%)
  starting transfers between devices  33.4 us (29%)
  Pallas kernels  29.1 us (26%)
  blocking collectives  10.8 us (9%)
  local copies, waits for them, and re-layouts  2.42 us (2%)
  other arithmetic  1.17 us (1%)
    ppermute x20, waiting for transfers between devices, swap(): lax.ppermute(rows, 'wide', [(i, i ^ mask) for i in range(count)])  35.2 us
    ppermute x20, starting transfers between devices, swap(): lax.ppermute(rows, 'wide', [(i, i ^ mask) for i in range(count)])  28.1 us
    all_to_all x1, blocking collectives, on_device(): lax.all_to_all(total.reshape(count, per, basis), 'wide', split_axis=0, co...  10.8 us
    pallas_call x1, Pallas kernels, weights(): pl.pallas_call(functools.partial(weights_kernel, sum(parts)), out_shape=j...  10.1 us
    pallas_call x1, Pallas kernels, contract(): pl.pallas_call(functools.partial(contract_kernel, parts, extra, groups, p...  9.8 us
    pallas_call x1, Pallas kernels, pack(): pl.pallas_call(functools.partial(pack_kernel, parts, extra, groups), out_...  6.32 us
    all_to_all x1, starting transfers between devices, share(): lax.all_to_all(packed, 'wide', split_axis=0, concat_axis=0, tiled=True)  5.29 us
  transfers between devices with their start and end apart: 21, of which 5 were waited for; matrix products, arithmetic and copies ran while one was open for 2% of the time, Pallas kernels for 16%

profile of v1, /device:TPU:0, one launch (start us, length us, event | category | flops | bytes accessed | tf_op | source)
XLA Modules:
  0.0 113.8 jit_solution(2663871368906897665)
XLA Ops:
  0.0 1.4 %choose.1 = s32[1]{0:T(128)} custom-call(s32[8,8]{1,0:T(8,128)} %pattern_ref.1), custom_call_target="tpu_custom_call" | custom-call | tf_op jit(solution)/shard_map/choose/pallas_call | solution.py:392
  2.0 100.3 %conditional.1 = (f32[128,128]{1,0:T(8,128)S(1)}) conditional(s32[]{:T(128)} %bitcast.138, (bf16[2048,4,128]{2,1,0:T(4,128)(2,1)}, bf16[2048,4,128]{2,1,0:T(4,128)(2,1)}, s32[8,8]{1,0:T(8,128)}, (), bf16[4,1024]{1,0:T(4,128)(2,1)}, /*index=5*/(), ()) %tuple.29, (bf16[2048,4,128]{2,1,0:T(4,128)(2,1)}, ...), branch_computations={%region_0.1_spmd, %region_1.2_spmd, %region_2.3_spmd, %region_3.4_... | conditional | flops 1946763392 | bytes 36578504 | solution.py:435
  2.3 4.1 %collective-permute-start.61 = (bf16[1,4,1024]{2,1,0:T(4,128)(2,1)}, bf16[1,4,1024]{2,1,0:T(4,128)(2,1)S(1)}, u32[]{:S(2)}, u32[]{:S(2)}) collective-permute-start(bf16[1,4,1024]{2,1,0:T(4,128)(2,1)} %bitcast.302), channel_id=1, source_target_pairs={{0,16},{1,17},{2,18},{3,19},{4,20},{5,21},{6,22},{7,23},{8,24},{9,... | collective-permute-start | bytes 24584 | tf_op jit(solution)/shard_map/cond/branch_4_fun/ppermute | solution.py:367
  6.4 1.3 %collective-permute-start.62 = (bf16[1,4,1024]{2,1,0:T(4,128)(2,1)}, bf16[1,4,1024]{2,1,0:T(4,128)(2,1)S(1)}, u32[]{:S(2)}, u32[]{:S(2)}) collective-permute-start(bf16[1,4,1024]{2,1,0:T(4,128)(2,1)} %bitcast.303), channel_id=1, source_target_pairs={{0,24},{1,25},{2,26},{3,27},{4,28},{5,29},{6,30},{7,31},{8,16},{9,... | collective-permute-start | bytes 24584 | tf_op jit(solution)/shard_map/cond/branch_4_fun/ppermute | solution.py:367
  7.7 0.2 collective-permute-start.60
  8.0 6.3 %pack.10 = (bf16[32,320,128]{2,1,0:T(8,128)(2,1)}, bf16[4,128,128]{2,1,0:T(8,128)(2,1)}, bf16[4,128,128]{2,1,0:T(8,128)(2,1)}, bf16[4,128,128]{2,1,0:T(8,128)(2,...) custom-call(s32[1]{0:T(128)} %bitcast.92.me_ref, ...), custom_call_target="tpu_custom_call" | custom-call | flops 1610612736 | bytes 7864320 | tf_op jit(solution)/shard_map/cond/branch_4_fun/pack/pallas_call | solution.py:146
  14.4 0.0 collective-permute-done.62
  14.4 0.0 collective-permute-done.60
  14.5 5.3 %all-to-all-start.4 = ((bf16[32,320,128]{2,1,0:T(8,128)(2,1)}), bf16[32,320,128]{2,1,0:T(8,128)(2,1)}, u32[]{:S(2)}, u32[]{:S(2)}) async-start(bf16[32,320,128]{2,1,0:T(8,128)(2,1)} %get-tuple-element.174), calls=%async_computation.4 | async-start | bytes 5242880 | tf_op jit(solution)/shard_map/cond/branch_4_fun/all_to_all | solution.py:415
  19.8 0.0 copy-start.5
  19.8 0.0 copy-start.26
  19.9 2.4 %collective-permute-start.69 = (bf16[4,4,1024]{2,1,0:T(4,128)(2,1)S(1)}, bf16[4,4,1024]{2,1,0:T(4,128)(2,1)S(1)}, u32[]{:S(2)}, u32[]{:S(2)}) collective-permute-start(bf16[4,4,1024]{2,1,0:T(4,128)(2,1)S(1)} %maximum_bitcast_fusion.4), channel_id=1, source_target_pairs={{0,7},{1,6},{2,5},{3,4},{4,3},{5,2},{6,1},{7,0},{8,15},{9,14},{10,... | collective-permute-start | bytes 98312 | tf_op jit(solution)/shard_map/cond/branch_4_fun/ppermute | solution.py:367
  22.3 0.4 collective-permute-start.68
  22.6 1.4 %collective-permute-start.67 = (bf16[4,4,1024]{2,1,0:T(4,128)(2,1)S(1)}, bf16[4,4,1024]{2,1,0:T(4,128)(2,1)S(1)}, u32[]{:S(2)}, u32[]{:S(2)}) collective-permute-start(bf16[4,4,1024]{2,1,0:T(4,128)(2,1)S(1)} %maximum_bitcast_fusion.4), channel_id=1, source_target_pairs={{0,5},{1,4},{2,7},{3,6},{4,1},{5,0},{6,3},{7,2},{8,13},{9,12},{10,... | collective-permute-start | bytes 98312 | tf_op jit(solution)/shard_map/cond/branch_4_fun/ppermute | solution.py:367
  24.0 0.4 collective-permute-start.66
  24.4 1.4 %collective-permute-start.65 = (bf16[4,4,1024]{2,1,0:T(4,128)(2,1)S(1)}, bf16[4,4,1024]{2,1,0:T(4,128)(2,1)S(1)}, u32[]{:S(2)}, u32[]{:S(2)}) collective-permute-start(bf16[4,4,1024]{2,1,0:T(4,128)(2,1)S(1)} %maximum_bitcast_fusion.4), channel_id=1, source_target_pairs={{0,3},{1,2},{2,1},{3,0},{4,7},{5,6},{6,5},{7,4},{8,11},{9,10},{10,... | collective-permute-start | bytes 98312 | tf_op jit(solution)/shard_map/cond/branch_4_fun/ppermute | solution.py:367
  25.8 12.0 %collective-permute-done.69 = bf16[4,4,1024]{2,1,0:T(4,128)(2,1)S(1)} collective-permute-done((bf16[4,4,1024]{2,1,0:T(4,128)(2,1)S(1)}, bf16[4,4,1024]{2,1,0:T(4,128)(2,1)S(1)}, u32[]{:S(2)}, u32[]{:S(2)}) %collective-permute-start.69) | collective-permute-done | bytes 32800 | tf_op jit(solution)/shard_map/cond/branch_4_fun/ppermute | solution.py:367
  37.8 3.2 %collective-permute-start.64 = (bf16[4,4,1024]{2,1,0:T(4,128)(2,1)S(1)}, bf16[4,4,1024]{2,1,0:T(4,128)(2,1)S(1)}, u32[]{:S(2)}, u32[]{:S(2)}) collective-permute-start(bf16[4,4,1024]{2,1,0:T(4,128)(2,1)S(1)} %maximum_bitcast_fusion.4), channel_id=1, source_target_pairs={{0,2},{1,3},{2,0},{3,1},{4,6},{5,7},{6,4},{7,5},{8,10},{9,11},{10,... | collective-permute-start | bytes 98312 | tf_op jit(solution)/shard_map/cond/branch_4_fun/ppermute | solution.py:367
  41.0 1.4 %collective-permute-start.63 = (bf16[4,4,1024]{2,1,0:T(4,128)(2,1)S(1)}, bf16[4,4,1024]{2,1,0:T(4,128)(2,1)S(1)}, u32[]{:S(2)}, u32[]{:S(2)}) collective-permute-start(bf16[4,4,1024]{2,1,0:T(4,128)(2,1)S(1)} %maximum_bitcast_fusion.4), channel_id=1, source_target_pairs={{0,1},{1,0},{2,3},{3,2},{4,5},{5,4},{6,7},{7,6},{8,9},{9,8},{10,11... | collective-permute-start | bytes 98312 | tf_op jit(solution)/shard_map/cond/branch_4_fun/ppermute | solution.py:367
  42.4 0.0 collective-permute-done.67
  42.4 0.1 collective-permute-start.70
  42.5 0.0 collective-permute-done.66
  42.5 2.4 %collective-permute-start.71 = (bf16[4,128,128]{2,1,0:T(8,128)(2,1)S(1)}, bf16[4,128,128]{2,1,0:T(8,128)(2,1)S(1)}, u32[]{:S(2)}, u32[]{:S(2)}) collective-permute-start(bf16[4,128,128]{2,1,0:T(8,128)(2,1)S(1)} %copy-done.38), channel_id=1, source_target_pairs={{0,2},{1,3},{2,0},{3,1},{4,6},{5,7},{6,4},{7,5},{8,10},{9,11},{10,... | collective-permute-start | bytes 393224 | tf_op jit(solution)/shard_map/cond/branch_4_fun/ppermute | solution.py:367
  45.0 0.0 collective-permute-start.72
  45.0 0.0 collective-permute-done.64
  45.0 1.4 %collective-permute-start.73 = (bf16[4,128,128]{2,1,0:T(8,128)(2,1)S(1)}, bf16[4,128,128]{2,1,0:T(8,128)(2,1)S(1)}, u32[]{:S(2)}, u32[]{:S(2)}) collective-permute-start(bf16[4,128,128]{2,1,0:T(8,128)(2,1)S(1)} %copy-done.34), channel_id=1, source_target_pairs={{0,4},{1,5},{2,6},{3,7},{4,0},{5,1},{6,2},{7,3},{8,12},{9,13},{10,... | collective-permute-start | bytes 393224 | tf_op jit(solution)/shard_map/cond/branch_4_fun/ppermute | solution.py:367
  46.4 0.4 collective-permute-start.74
  46.8 0.1 constant_dynamic-update-slice_fusion.23
  46.9 0.1 constant_dynamic-update-slice_fusion.22
  47.1 0.1 constant_dynamic-update-slice_fusion.20
  47.2 0.1 constant_dynamic-update-slice_fusion.18
  47.3 1.5 %collective-permute-start.75 = (bf16[4,128,128]{2,1,0:T(8,128)(2,1)S(1)}, bf16[4,128,128]{2,1,0:T(8,128)(2,1)S(1)}, u32[]{:S(2)}, u32[]{:S(2)}) collective-permute-start(bf16[4,128,128]{2,1,0:T(8,128)(2,1)S(1)} %copy-done.30), channel_id=1, source_target_pairs={{0,6},{1,7},{2,4},{3,5},{4,2},{5,3},{6,0},{7,1},{8,14},{9,15},{10,... | collective-permute-start | bytes 393224 | tf_op jit(solution)/shard_map/cond/branch_4_fun/ppermute | solution.py:367
  48.8 8.0 %collective-permute-done.71 = bf16[4,128,128]{2,1,0:T(8,128)(2,1)S(1)} collective-permute-done((bf16[4,128,128]{2,1,0:T(8,128)(2,1)S(1)}, bf16[4,128,128]{2,1,0:T(8,128)(2,1)S(1)}, u32[]{:S(2)}, u32[]{:S(2)}) %collective-permute-start.71) | collective-permute-done | bytes 131104 | tf_op jit(solution)/shard_map/cond/branch_4_fun/ppermute | solution.py:367
  56.9 2.2 %collective-permute-done.72 = bf16[4,128,128]{2,1,0:T(8,128)(2,1)S(1)} collective-permute-done((bf16[4,128,128]{2,1,0:T(8,128)(2,1)S(1)}, bf16[4,128,128]{2,1,0:T(8,128)(2,1)S(1)}, u32[]{:S(2)}, u32[]{:S(2)}) %collective-permute-start.72) | collective-permute-done | bytes 131104 | tf_op jit(solution)/shard_map/cond/branch_4_fun/ppermute | solution.py:367
  59.2 5.5 %collective-permute-done.74 = bf16[4,128,128]{2,1,0:T(8,128)(2,1)S(1)} collective-permute-done((bf16[4,128,128]{2,1,0:T(8,128)(2,1)S(1)}, bf16[4,128,128]{2,1,0:T(8,128)(2,1)S(1)}, u32[]{:S(2)}, u32[]{:S(2)}) %collective-permute-start.74) | collective-permute-done | bytes 131104 | tf_op jit(solution)/shard_map/cond/branch_4_fun/ppermute | solution.py:367
  64.8 1.5 %sort.5 = bf16[4,4,128,128]{3,2,1,0:T(8,128)(2,1)S(1)} custom-call(s32[1]{0:T(128)} %bitcast.92.me_ref, s32[8,8]{1,0:T(8,128)S(1)} %copy-done.5, s32[3,128]{1,0:T(4,128)S(1)} %copy-done.26, bf16[8,4,128,128]{3,2,1,0:T(8,128)(2,1)S(1)} %bitcast_dynamic-update-slice_fusion.32.over_ref), custom_call_target="tpu_custom_call" | custom-call | flops 134217728 | bytes 2097152 | tf_op jit(solution)/shard_map/cond/branch_4_fun/sort/pallas_call | solution.py:197
  66.3 0.7 slice_bitcast_fusion.8
  67.0 4.9 %collective-permute-start.79 = (bf16[4,128,128]{2,1,0:T(8,128)(2,1)S(1)}, bf16[4,128,128]{2,1,0:T(8,128)(2,1)S(1)}, u32[]{:S(2)}, u32[]{:S(2)}) collective-permute-start(bf16[4,128,128]{2,1,0:T(8,128)(2,1)S(1)} %get-tuple-element.302), channel_id=1, source_target_pairs={{0,24},{1,25},{2,26},{3,27},{4,28},{5,29},{6,30},{7,31},{8,16},{9,... | collective-permute-start | bytes 393224 | tf_op jit(solution)/shard_map/cond/branch_4_fun/ppermute | solution.py:367
  71.9 1.1 collective-permute-start.78
  73.1 0.1 copy.37
  73.2 0.8 reshape.89.panel_ref
  73.9 10.1 %weights.10.tables_hbm = bf16[8,768,256]{2,1,0:T(8,128)(2,1)} custom-call(s32[8,8]{1,0:T(8,128)S(1)} %copy-done.5, s32[384,3]{1,0:T(8,128)} %constant.537.clone.1.layout_ref, bf16[128,1024]{1,0:T(8,128)(2,1)} %reshape.89.panel_ref), custom_call_target="tpu_custom_call" | custom-call | flops 201326592 | bytes 524288 | tf_op jit(solution)/shard_map/cond/branch_4_fun/weights/pallas_call | solution.py:236
  84.1 7.5 %collective-permute-done.78.refs_2_ = bf16[4,128,128]{2,1,0:T(8,128)(2,1)S(1)} collective-permute-done((bf16[4,128,128]{2,1,0:T(8,128)(2,1)S(1)}, bf16[4,128,128]{2,1,0:T(8,128)(2,1)S(1)}, u32[]{:S(2)}, u32[]{:S(2)}) %collective-permute-start.78) | collective-permute-done | bytes 131104 | tf_op jit(solution)/shard_map/cond/branch_4_fun/ppermute | solution.py:367
  91.6 0.6 copy-done.16
  92.2 0.1 copy-done.18
  92.2 9.8 %contract.10 = f32[128,128]{1,0:T(8,128)S(1)} custom-call(s32[1]{0:T(128)} %bitcast.92.me_ref, bf16[8,768,256]{2,1,0:T(8,128)(2,1)} %weights.10.tables_hbm, bf16[32,320,128]{2,1,0:T(8,128)(2,1)} %all-to-all-done.4.got_hbm, bf16[4,128,128]{2,1,0:T(8,128)(2,1)} %get-tuple-element.305.refs_0_, bf16[4,128,128]{2,1,0:T(8,128)(2,1)} %copy-done.18, ...), custom_call_target="tpu_custom_call" | custom-call | tf_op jit(solution)/shard_map/cond/branch_4_fun/contract/pallas_call | solution.py:347
  102.4 10.8 %all_to_all.29 = f32[32,4,128]{2,1,0:T(4,128)S(1)} all-to-all(f32[32,4,128]{2,1,0:T(4,128)S(1)} %bitcast.308), channel_id=1, replica_groups=mesh['wide'=32,'narrow'=1] {'wide'}, dimensions={0} | all-to-all | bytes 131072 | tf_op jit(solution)/shard_map/all_to_all | solution.py:436
  113.1 0.6 reduce_sum.9
  (51 shorter events, 0.5 us)
Async XLA Ops:
  2.3 12.1 %collective-permute-start.61 = (bf16[1,4,1024]{2,1,0:T(4,128)(2,1)}, bf16[1,4,1024]{2,1,0:T(4,128)(2,1)S(1)}, u32[]{:S(2)}, u32[]{:S(2)}) collective-permute-start(bf16[1,4,1024]{2,1,0:T(4,128)(2,1)} %bitcast.302), channel_id=1, source_target_pairs={{0,16},{1,17},{2,18},{3,19},{4,20},{5,21},{6,22},{7,23},{8,24},{9,... | collective-permute-start | bytes 24584 | tf_op jit(solution)/shard_map/cond/branch_4_fun/ppermute | solution.py:367
  6.4 8.0 %collective-permute-start.62 = (bf16[1,4,1024]{2,1,0:T(4,128)(2,1)}, bf16[1,4,1024]{2,1,0:T(4,128)(2,1)S(1)}, u32[]{:S(2)}, u32[]{:S(2)}) collective-permute-start(bf16[1,4,1024]{2,1,0:T(4,128)(2,1)} %bitcast.303), channel_id=1, source_target_pairs={{0,24},{1,25},{2,26},{3,27},{4,28},{5,29},{6,30},{7,31},{8,16},{9,... | collective-permute-start | bytes 24584 | tf_op jit(solution)/shard_map/cond/branch_4_fun/ppermute | solution.py:367
  7.7 6.6 %collective-permute-start.60 = (bf16[1,4,1024]{2,1,0:T(4,128)(2,1)}, bf16[1,4,1024]{2,1,0:T(4,128)(2,1)S(1)}, u32[]{:S(2)}, u32[]{:S(2)}) collective-permute-start(bf16[1,4,1024]{2,1,0:T(4,128)(2,1)} %bitcast.304), channel_id=1, source_target_pairs={{0,8},{1,9},{2,10},{3,11},{4,12},{5,13},{6,14},{7,15},{8,0},{9,1},... | collective-permute-start | bytes 24584 | tf_op jit(solution)/shard_map/cond/branch_4_fun/ppermute | solution.py:367
  8.0 6.4 %copy-start.11 = (bf16[4,1024]{1,0:T(4,128)(2,1)S(1)}, bf16[4,1024]{1,0:T(4,128)(2,1)}, u32[]{:S(2)}) copy-start(bf16[4,1024]{1,0:T(4,128)(2,1)} %get-tuple-element.164) | copy-start | bytes 24580 | tf_op jit(solution)/shard_map/cond
  14.5 28.0 %copy-start.20 = (bf16[4,128,128]{2,1,0:T(8,128)(2,1)S(1)}, bf16[4,128,128]{2,1,0:T(8,128)(2,1)}, u32[]{:S(2)}) copy-start(bf16[4,128,128]{2,1,0:T(8,128)(2,1)} %get-tuple-element.176) | copy-start | bytes 393220 | tf_op jit(solution)/shard_map/cond
  14.5 28.0 %copy-start.40 = (bf16[4,128,128]{2,1,0:T(8,128)(2,1)S(1)}, bf16[4,128,128]{2,1,0:T(8,128)(2,1)}, u32[]{:S(2)}) copy-start(bf16[4,128,128]{2,1,0:T(8,128)(2,1)} %get-tuple-element.177) | copy-start | bytes 393220 | tf_op jit(solution)/shard_map/cond
  14.5 28.1 %copy-start.38 = (bf16[4,128,128]{2,1,0:T(8,128)(2,1)S(1)}, bf16[4,128,128]{2,1,0:T(8,128)(2,1)}, u32[]{:S(2)}) copy-start(bf16[4,128,128]{2,1,0:T(8,128)(2,1)} %get-tuple-element.178) | copy-start | bytes 393220 | tf_op jit(solution)/shard_map/cond
  14.5 30.5 %copy-start.36 = (bf16[4,128,128]{2,1,0:T(8,128)(2,1)S(1)}, bf16[4,128,128]{2,1,0:T(8,128)(2,1)}, u32[]{:S(2)}) copy-start(bf16[4,128,128]{2,1,0:T(8,128)(2,1)} %get-tuple-element.179) | copy-start | bytes 393220 | tf_op jit(solution)/shard_map/cond
  14.5 30.5 %copy-start.34 = (bf16[4,128,128]{2,1,0:T(8,128)(2,1)S(1)}, bf16[4,128,128]{2,1,0:T(8,128)(2,1)}, u32[]{:S(2)}) copy-start(bf16[4,128,128]{2,1,0:T(8,128)(2,1)} %get-tuple-element.180) | copy-start | bytes 393220 | tf_op jit(solution)/shard_map/cond
  14.5 31.9 %copy-start.32 = (bf16[4,128,128]{2,1,0:T(8,128)(2,1)S(1)}, bf16[4,128,128]{2,1,0:T(8,128)(2,1)}, u32[]{:S(2)}) copy-start(bf16[4,128,128]{2,1,0:T(8,128)(2,1)} %get-tuple-element.181) | copy-start | bytes 393220 | tf_op jit(solution)/shard_map/cond
  14.5 32.8 %copy-start.30 = (bf16[4,128,128]{2,1,0:T(8,128)(2,1)S(1)}, bf16[4,128,128]{2,1,0:T(8,128)(2,1)}, u32[]{:S(2)}) copy-start(bf16[4,128,128]{2,1,0:T(8,128)(2,1)} %get-tuple-element.182) | copy-start | bytes 393220 | tf_op jit(solution)/shard_map/cond
  14.5 77.0 %all-to-all-start.4 = ((bf16[32,320,128]{2,1,0:T(8,128)(2,1)}), bf16[32,320,128]{2,1,0:T(8,128)(2,1)}, u32[]{:S(2)}, u32[]{:S(2)}) async-start(bf16[32,320,128]{2,1,0:T(8,128)(2,1)} %get-tuple-element.174), calls=%async_computation.4 | async-start | bytes 5242880 | tf_op jit(solution)/shard_map/cond/branch_4_fun/all_to_all | solution.py:415
  19.8 37.0 %copy-start.28 = (bf16[4,128,128]{2,1,0:T(8,128)(2,1)S(1)}, bf16[4,128,128]{2,1,0:T(8,128)(2,1)}, u32[]{:S(2)}) copy-start(bf16[4,128,128]{2,1,0:T(8,128)(2,1)} %get-tuple-element.183) | copy-start | bytes 393220 | tf_op jit(solution)/shard_map/cond
  19.8 45.0 %copy-start.5 = (s32[8,8]{1,0:T(8,128)S(1)}, s32[8,8]{1,0:T(8,128)}, u32[]{:S(2)}) copy-start(s32[8,8]{1,0:T(8,128)} %get-tuple-element.158.pattern_ref) | copy-start | bytes 772 | tf_op jit(solution)/shard_map/cond
  19.8 44.9 %copy-start.26 = (s32[3,128]{1,0:T(4,128)S(1)}, s32[3,128]{1,0:T(4,128)}, u32[]{:S(2)}) copy-start(s32[3,128]{1,0:T(4,128)} %get-tuple-element.175.slot_ref) | copy-start | bytes 4612 | tf_op jit(solution)/shard_map/cond
  19.9 17.9 %collective-permute-start.69 = (bf16[4,4,1024]{2,1,0:T(4,128)(2,1)S(1)}, bf16[4,4,1024]{2,1,0:T(4,128)(2,1)S(1)}, u32[]{:S(2)}, u32[]{:S(2)}) collective-permute-start(bf16[4,4,1024]{2,1,0:T(4,128)(2,1)S(1)} %maximum_bitcast_fusion.4), channel_id=1, source_target_pairs={{0,7},{1,6},{2,5},{3,4},{4,3},{5,2},{6,1},{7,0},{8,15},{9,14},{10,... | collective-permute-start | bytes 98312 | tf_op jit(solution)/shard_map/cond/branch_4_fun/ppermute | solution.py:367
  22.3 18.7 %collective-permute-start.68 = (bf16[4,4,1024]{2,1,0:T(4,128)(2,1)S(1)}, bf16[4,4,1024]{2,1,0:T(4,128)(2,1)S(1)}, u32[]{:S(2)}, u32[]{:S(2)}) collective-permute-start(bf16[4,4,1024]{2,1,0:T(4,128)(2,1)S(1)} %maximum_bitcast_fusion.4), channel_id=1, source_target_pairs={{0,6},{1,7},{2,4},{3,5},{4,2},{5,3},{6,0},{7,1},{8,14},{9,15},{10,... | collective-permute-start | bytes 98312 | tf_op jit(solution)/shard_map/cond/branch_4_fun/ppermute | solution.py:367
  22.6 19.8 %collective-permute-start.67 = (bf16[4,4,1024]{2,1,0:T(4,128)(2,1)S(1)}, bf16[4,4,1024]{2,1,0:T(4,128)(2,1)S(1)}, u32[]{:S(2)}, u32[]{:S(2)}) collective-permute-start(bf16[4,4,1024]{2,1,0:T(4,128)(2,1)S(1)} %maximum_bitcast_fusion.4), channel_id=1, source_target_pairs={{0,5},{1,4},{2,7},{3,6},{4,1},{5,0},{6,3},{7,2},{8,13},{9,12},{10,... | collective-permute-start | bytes 98312 | tf_op jit(solution)/shard_map/cond/branch_4_fun/ppermute | solution.py:367
  24.0 18.5 %collective-permute-start.66 = (bf16[4,4,1024]{2,1,0:T(4,128)(2,1)S(1)}, bf16[4,4,1024]{2,1,0:T(4,128)(2,1)S(1)}, u32[]{:S(2)}, u32[]{:S(2)}) collective-permute-start(bf16[4,4,1024]{2,1,0:T(4,128)(2,1)S(1)} %maximum_bitcast_fusion.4), channel_id=1, source_target_pairs={{0,4},{1,5},{2,6},{3,7},{4,0},{5,1},{6,2},{7,3},{8,12},{9,13},{10,... | collective-permute-start | bytes 98312 | tf_op jit(solution)/shard_map/cond/branch_4_fun/ppermute | solution.py:367
  24.4 20.6 %collective-permute-start.65 = (bf16[4,4,1024]{2,1,0:T(4,128)(2,1)S(1)}, bf16[4,4,1024]{2,1,0:T(4,128)(2,1)S(1)}, u32[]{:S(2)}, u32[]{:S(2)}) collective-permute-start(bf16[4,4,1024]{2,1,0:T(4,128)(2,1)S(1)} %maximum_bitcast_fusion.4), channel_id=1, source_target_pairs={{0,3},{1,2},{2,1},{3,0},{4,7},{5,6},{6,5},{7,4},{8,11},{9,10},{10,... | collective-permute-start | bytes 98312 | tf_op jit(solution)/shard_map/cond/branch_4_fun/ppermute | solution.py:367
  37.8 7.2 %collective-permute-start.64 = (bf16[4,4,1024]{2,1,0:T(4,128)(2,1)S(1)}, bf16[4,4,1024]{2,1,0:T(4,128)(2,1)S(1)}, u32[]{:S(2)}, u32[]{:S(2)}) collective-permute-start(bf16[4,4,1024]{2,1,0:T(4,128)(2,1)S(1)} %maximum_bitcast_fusion.4), channel_id=1, source_target_pairs={{0,2},{1,3},{2,0},{3,1},{4,6},{5,7},{6,4},{7,5},{8,10},{9,11},{10,... | collective-permute-start | bytes 98312 | tf_op jit(solution)/shard_map/cond/branch_4_fun/ppermute | solution.py:367
  41.0 5.4 %collective-permute-start.63 = (bf16[4,4,1024]{2,1,0:T(4,128)(2,1)S(1)}, bf16[4,4,1024]{2,1,0:T(4,128)(2,1)S(1)}, u32[]{:S(2)}, u32[]{:S(2)}) collective-permute-start(bf16[4,4,1024]{2,1,0:T(4,128)(2,1)S(1)} %maximum_bitcast_fusion.4), channel_id=1, source_target_pairs={{0,1},{1,0},{2,3},{3,2},{4,5},{5,4},{6,7},{7,6},{8,9},{9,8},{10,11... | collective-permute-start | bytes 98312 | tf_op jit(solution)/shard_map/cond/branch_4_fun/ppermute | solution.py:367
  42.4 4.8 %collective-permute-start.70 = (bf16[4,128,128]{2,1,0:T(8,128)(2,1)S(1)}, bf16[4,128,128]{2,1,0:T(8,128)(2,1)S(1)}, u32[]{:S(2)}, u32[]{:S(2)}) collective-permute-start(bf16[4,128,128]{2,1,0:T(8,128)(2,1)S(1)} %copy-done.40), channel_id=1, source_target_pairs={{0,1},{1,0},{2,3},{3,2},{4,5},{5,4},{6,7},{7,6},{8,9},{9,8},{10,11... | collective-permute-start | bytes 393224 | tf_op jit(solution)/shard_map/cond/branch_4_fun/ppermute | solution.py:367
  42.5 14.3 %collective-permute-start.71 = (bf16[4,128,128]{2,1,0:T(8,128)(2,1)S(1)}, bf16[4,128,128]{2,1,0:T(8,128)(2,1)S(1)}, u32[]{:S(2)}, u32[]{:S(2)}) collective-permute-start(bf16[4,128,128]{2,1,0:T(8,128)(2,1)S(1)} %copy-done.38), channel_id=1, source_target_pairs={{0,2},{1,3},{2,0},{3,1},{4,6},{5,7},{6,4},{7,5},{8,10},{9,11},{10,... | collective-permute-start | bytes 393224 | tf_op jit(solution)/shard_map/cond/branch_4_fun/ppermute | solution.py:367
  45.0 14.1 %collective-permute-start.72 = (bf16[4,128,128]{2,1,0:T(8,128)(2,1)S(1)}, bf16[4,128,128]{2,1,0:T(8,128)(2,1)S(1)}, u32[]{:S(2)}, u32[]{:S(2)}) collective-permute-start(bf16[4,128,128]{2,1,0:T(8,128)(2,1)S(1)} %copy-done.36), channel_id=1, source_target_pairs={{0,3},{1,2},{2,1},{3,0},{4,7},{5,6},{6,5},{7,4},{8,11},{9,10},{10,... | collective-permute-start | bytes 393224 | tf_op jit(solution)/shard_map/cond/branch_4_fun/ppermute | solution.py:367
  45.0 14.1 %collective-permute-start.73 = (bf16[4,128,128]{2,1,0:T(8,128)(2,1)S(1)}, bf16[4,128,128]{2,1,0:T(8,128)(2,1)S(1)}, u32[]{:S(2)}, u32[]{:S(2)}) collective-permute-start(bf16[4,128,128]{2,1,0:T(8,128)(2,1)S(1)} %copy-done.34), channel_id=1, source_target_pairs={{0,4},{1,5},{2,6},{3,7},{4,0},{5,1},{6,2},{7,3},{8,12},{9,13},{10,... | collective-permute-start | bytes 393224 | tf_op jit(solution)/shard_map/cond/branch_4_fun/ppermute | solution.py:367
  46.4 18.2 %collective-permute-start.74 = (bf16[4,128,128]{2,1,0:T(8,128)(2,1)S(1)}, bf16[4,128,128]{2,1,0:T(8,128)(2,1)S(1)}, u32[]{:S(2)}, u32[]{:S(2)}) collective-permute-start(bf16[4,128,128]{2,1,0:T(8,128)(2,1)S(1)} %copy-done.32), channel_id=1, source_target_pairs={{0,5},{1,4},{2,7},{3,6},{4,1},{5,0},{6,3},{7,2},{8,13},{9,12},{10,... | collective-permute-start | bytes 393224 | tf_op jit(solution)/shard_map/cond/branch_4_fun/ppermute | solution.py:367
  47.3 17.4 %collective-permute-start.75 = (bf16[4,128,128]{2,1,0:T(8,128)(2,1)S(1)}, bf16[4,128,128]{2,1,0:T(8,128)(2,1)S(1)}, u32[]{:S(2)}, u32[]{:S(2)}) collective-permute-start(bf16[4,128,128]{2,1,0:T(8,128)(2,1)S(1)} %copy-done.30), channel_id=1, source_target_pairs={{0,6},{1,7},{2,4},{3,5},{4,2},{5,3},{6,0},{7,1},{8,14},{9,15},{10,... | collective-permute-start | bytes 393224 | tf_op jit(solution)/shard_map/cond/branch_4_fun/ppermute | solution.py:367
  56.8 7.9 %collective-permute-start.76 = (bf16[4,128,128]{2,1,0:T(8,128)(2,1)S(1)}, bf16[4,128,128]{2,1,0:T(8,128)(2,1)S(1)}, u32[]{:S(2)}, u32[]{:S(2)}) collective-permute-start(bf16[4,128,128]{2,1,0:T(8,128)(2,1)S(1)} %copy-done.28), channel_id=1, source_target_pairs={{0,7},{1,6},{2,5},{3,4},{4,3},{5,2},{6,1},{7,0},{8,15},{9,14},{10,... | collective-permute-start | bytes 393224 | tf_op jit(solution)/shard_map/cond/branch_4_fun/ppermute | solution.py:367
  67.0 17.1 %collective-permute-start.79 = (bf16[4,128,128]{2,1,0:T(8,128)(2,1)S(1)}, bf16[4,128,128]{2,1,0:T(8,128)(2,1)S(1)}, u32[]{:S(2)}, u32[]{:S(2)}) collective-permute-start(bf16[4,128,128]{2,1,0:T(8,128)(2,1)S(1)} %get-tuple-element.302), channel_id=1, source_target_pairs={{0,24},{1,25},{2,26},{3,27},{4,28},{5,29},{6,30},{7,31},{8,16},{9,... | collective-permute-start | bytes 393224 | tf_op jit(solution)/shard_map/cond/branch_4_fun/ppermute | solution.py:367
  71.9 19.6 %collective-permute-start.78 = (bf16[4,128,128]{2,1,0:T(8,128)(2,1)S(1)}, bf16[4,128,128]{2,1,0:T(8,128)(2,1)S(1)}, u32[]{:S(2)}, u32[]{:S(2)}) collective-permute-start(bf16[4,128,128]{2,1,0:T(8,128)(2,1)S(1)} %get-tuple-element.303), channel_id=1, source_target_pairs={{0,16},{1,17},{2,18},{3,19},{4,20},{5,21},{6,22},{7,23},{8,24},{9,... | collective-permute-start | bytes 393224 | tf_op jit(solution)/shard_map/cond/branch_4_fun/ppermute | solution.py:367
  73.0 18.5 %collective-permute-start.77 = (bf16[4,128,128]{2,1,0:T(8,128)(2,1)S(1)}, bf16[4,128,128]{2,1,0:T(8,128)(2,1)S(1)}, u32[]{:S(2)}, u32[]{:S(2)}) collective-permute-start(bf16[4,128,128]{2,1,0:T(8,128)(2,1)S(1)} %get-tuple-element.304), channel_id=1, source_target_pairs={{0,8},{1,9},{2,10},{3,11},{4,12},{5,13},{6,14},{7,15},{8,0},{9,1},... | collective-permute-start | bytes 393224 | tf_op jit(solution)/shard_map/cond/branch_4_fun/ppermute | solution.py:367
  84.1 7.5 %copy-start.14 = (bf16[4,128,128]{2,1,0:T(8,128)(2,1)}, bf16[4,128,128]{2,1,0:T(8,128)(2,1)S(1)}, u32[]{:S(2)}) copy-start(bf16[4,128,128]{2,1,0:T(8,128)(2,1)S(1)} %collective-permute-done.79.refs_3_) | copy-start | bytes 393220 | tf_op jit(solution)/shard_map/cond
  91.5 0.6 copy-start.16
  91.5 0.7 copy-start.18
